TPU v7x, 32 devices: a whole 2x2x4 slice. The times are simulated.
32 devices in a mesh: box: 8 (over z, x), param: 4 (over y, core).
Axes of the slice: x: 2, y: 2, z: 4, core: 2. Of those that a mesh axis runs over, the one named last changes fastest.
Arguments:
- traces: float32 [8, 4, 512, 256], P('box', 'param'), may hold values from -6 to 6
- owners: int32 [8, 4, 512, 1], P('box', 'param'), may hold values from 0 to 3; in each aligned block of 512 rows (0 to 511, 512 to 1023, ..., all dimensions but the last counted through in order) at most 256 rows name the same one
- counts: int32 [8, 4], P('box', 'param'), may hold values from 128 to 512, as said below
- pair_table: int32 [8, 4, 4, 256], P('box', 'param'), may hold values from 0 to 511
- anterp: float32 [256, 512], replicated, may hold values from -0.375 to 0.375
- interp: float32 [2, 512, 256], replicated, may hold values from -0.25 to 0.25
- phase: float32 [8, 4, 3, 512, 256], P('box', 'param'), may hold values from -3.140625 to 3.140625
Outputs:
- weights_out: float32 [8, 4, 2, 512, 256], P('box', 'param')
Inputs may be any that keep to these rules, and one draw needn't show every extreme that they name: `owners`: in the 512 rows of one device no owner is named more than 256 times, a bound that some block reaches. `counts`: some device has all 512 blocks live in every draw.
All inputs are finite; a program needn't handle non-finite values.
Results may differ from a plain program's by a relative error of at most 0.00011.
Values sent between devices are 32-bit elements; how exact they have to be, the bound alone decides.
A program may use at most 64 MiB of HBM per device.

v0:
```python
import jax
import jax.numpy as jnp
from jax import lax
from jax.sharding import PartitionSpec as P

LEVELS = 3


HIGH = lax.Precision.HIGHEST


def swapped(x, axis, bit):
    return lax.ppermute(x, axis, [(i, i ^ 1 << bit) for i in range(lax.axis_size(axis))])


def rotate(weights_now, angles):
    cosine = jnp.cos(angles)
    sine_part = jnp.sin(angles)
    real_part = weights_now[0]
    imag_part = weights_now[1]
    return jnp.stack(
        [real_part * cosine - imag_part * sine_part, real_part * sine_part + imag_part * cosine],
        axis=0,
    )


def shards(traces, owners, counts, pair_table, anterp, interp, phase):
    blocks = traces[0, 0]
    destination = owners[0, 0, :, 0]
    live_count = counts[0, 0]
    param_count = lax.axis_size("param")
    slot_count = pair_table.shape[3]
    block_count = blocks.shape[0]
    weight_count = interp.shape[2]
    pair_count = phase.shape[3]
    live_mask = (jnp.arange(block_count, dtype=jnp.int32) < live_count).astype(jnp.float32)
    onehot = (destination[:, None] == jnp.arange(param_count, dtype=jnp.int32)[None, :]).astype(
        jnp.int32
    )
    ranking = jnp.sum((jnp.cumsum(onehot, axis=0) - onehot) * onehot, axis=1)
    position = destination * slot_count + ranking
    masked = blocks * live_mask[:, None]
    pair_ids = pair_table[0, 0].reshape(-1)
    selector = (jnp.arange(pair_count, dtype=jnp.int32)[:, None] == pair_ids[None, :]).astype(
        jnp.float32
    )
    coefficient = jnp.dot(masked, anterp, precision=HIGH)
    outgoing = (
        jnp.zeros((param_count * slot_count, 2 * weight_count), jnp.float32)
        .at[position]
        .set(coefficient)
    )
    arrived = lax.all_to_all(
        outgoing.reshape(param_count, slot_count, 2 * weight_count),
        "param",
        split_axis=0,
        concat_axis=0,
        tiled=True,
    )
    initial = jnp.dot(selector, arrived.reshape(-1, 2 * weight_count), precision=HIGH)
    weights_now = initial.reshape(pair_count, 2, weight_count).transpose(1, 0, 2)
    half_rows = pair_count // 2
    box_index = lax.axis_index("box")
    for level_id in range(LEVELS):
        side_bit = box_index >> level_id & 1
        kept_rows = lax.dynamic_slice_in_dim(weights_now, side_bit * half_rows, half_rows, 1)
        sent_rows = lax.dynamic_slice_in_dim(weights_now, (1 - side_bit) * half_rows, half_rows, 1)
        partner = swapped(sent_rows, "box", level_id)
        lower_rows = jnp.where(side_bit == 0, kept_rows, partner)
        upper_rows = jnp.where(side_bit == 0, partner, kept_rows)
        joined = jnp.concatenate([lower_rows, upper_rows], axis=2)
        combined = jnp.einsum("rqk,skj->rsqj", joined, interp, precision=HIGH).reshape(
            2, pair_count, weight_count
        )
        weights_now = rotate(combined, phase[0, 0, level_id])
    return weights_now[None, None]


def solution(mesh):
    placed = (
        P("box", "param", None, None),
        P("box", "param", None, None),
        P("box", "param"),
        P("box", "param", None, None),
        P(),
        P(),
        P("box", "param", None, None, None),
    )
    return jax.shard_map(
        shards,
        mesh=mesh,
        in_specs=placed,
        out_specs=P("box", "param", None, None, None),
        check_vma=False,
    )
```

profile of v0, /device:TPU:0, one launch (start us, length us, event | category | flops | bytes accessed | tf_op | source)
XLA Modules:
  0.0 114.6 jit_solution(13032445018192123971)
XLA Ops:
  0.0 0.8 fusion.30
  0.8 1.2 %reduce-window.6 = s32[4,4,128]{2,1,0:T(4,128)S(1)} reduce-window(s32[4,4,128]{2,1,0:T(4,128)S(1)} %fusion.30, s32[]{:T(128)} %constant.6.clone.1), window={size=1x1x128 pad=0_0x0_0x127_0}, to_apply=%region_0.0 | reduce-window | flops 260096 | bytes 16388 | tf_op jit(solution)/shard_map/reduce-window
  2.0 0.2 slice_reduce_fusion
  2.2 0.2 reduce-window.9
  2.4 0.1 add_bitcast_fusion
  2.5 0.7 fusion.29
  3.2 0.7 compare_select_fusion
  4.5 2.2 %fusion.25 = f32[512,512]{1,0:T(8,128)S(1)} fusion(f32[256,512]{1,0:T(8,128)} %param.11, f32[1,1,512,256]{3,2,1,0:T(8,128)} %param.7, f32[512]{0:T(512)S(1)} %fusion.31), kind=kOutput, calls=%fused_computation.56 | convolution fusion | flops 805437440 | bytes 2099200 | tf_op jit(solution)/shard_map/dot_general | solution.py:47
  6.8 3.7 %scatter_custom_fusion = f32[1024,512]{1,0:T(8,128)} fusion(s32[512]{0:T(512)S(1)} %bitcast.148, f32[512,512]{1,0:T(8,128)S(1)} %fusion.25, f32[]{:T(128)} %constant.7.clone.1), kind=kCustom, calls=%fused_computation.28 | custom fusion | bytes 2097156 | tf_op jit(solution)/shard_map/scatter | solution.py:51
  10.4 4.4 %all-to-all-start = ((f32[4,256,512]{2,1,0:T(8,128)}), f32[4,256,512]{2,1,0:T(8,128)S(1)}, u32[]{:S(2)}, u32[]{:S(2)}) async-start(f32[4,256,512]{2,1,0:T(8,128)} %bitcast.140), calls=%async_computation | async-start | bytes 4194304 | tf_op jit(solution)/shard_map/all_to_all | solution.py:53
  14.8 25.8 %all-to-all-done = f32[4,256,512]{2,1,0:T(8,128)S(1)} async-done(((f32[4,256,512]{2,1,0:T(8,128)}), f32[4,256,512]{2,1,0:T(8,128)S(1)}, u32[]{:S(2)}, u32[]{:S(2)}) %all-to-all-start) | async-done | bytes 2097184 | tf_op jit(solution)/shard_map/all_to_all | solution.py:53
  40.6 1.9 %copy.14 = f32[1024,512]{0,1:T(8,128)} copy(f32[1024,512]{1,0:T(8,128)S(1)} %bitcast.139) | data formatting | bytes 4194304 | tf_op jit(solution)/shard_map/reshape | solution.py:60
  42.5 3.5 %fusion.1 = f32[512,2,256]{0,2,1:T(8,128)S(1)} fusion(f32[2,256,1024]{2,1,0:T(8,128)} %bitcast.141, s32[1024]{0:T(1024)S(1)} %bitcast.147), kind=kOutput, calls=%fused_computation.3 | convolution fusion | flops 3221749760 | bytes 3149824 | tf_op jit(solution)/shard_map/dot_general | solution.py:60
  46.1 2.2 %collective-permute-start = (f32[2,256,256]{1,2,0:T(8,128)S(1)}, f32[2,256,256]{1,2,0:T(8,128)S(1)}, u32[]{:S(2)}, u32[]{:S(2)}) collective-permute-start(f32[2,256,256]{1,2,0:T(8,128)S(1)} %dynamic-slice_bitcast_fusion), channel_id=1, source_target_pairs={{0,4},{4,0},{8,12},{12,8},{16,20},{20,16},{24,28},{28,24},{1,5},{5... | collective-permute-start | bytes 1572872 | tf_op jit(solution)/shard_map/ppermute | solution.py:13
  48.3 11.7 %collective-permute-done = f32[2,256,256]{1,2,0:T(8,128)S(1)} collective-permute-done((f32[2,256,256]{1,2,0:T(8,128)S(1)}, f32[2,256,256]{1,2,0:T(8,128)S(1)}, u32[]{:S(2)}, u32[]{:S(2)}) %collective-permute-start) | collective-permute-done | bytes 524320 | tf_op jit(solution)/shard_map/ppermute | solution.py:13
  60.0 0.1 bitcast_select_fusion.1
  60.2 1.8 %convolution_bitcast_fusion.2 = f32[2,2,256,256]{3,2,1,0:T(8,128)S(1)} fusion(f32[2,256,256]{1,2,0:T(8,128)S(1)} %get-tuple-element.16, f32[2,256,256]{1,2,0:T(8,128)S(1)} %get-tuple-element.15, f32[2,512,256]{2,1,0:T(8,128)S(1)} %copy-done), kind=kOutput, calls=%fused_computation.6 | convolution fusion | flops 1610874880 | bytes 3145728 | tf_op jit(solution)/shard_map/rqk,skj->rsqj/dot_general | solution.py:72
  62.0 0.1 fusion.37
  62.1 3.4 %fusion.24 = (f32[1,512,256]{2,1,0:T(8,128)S(1)}, f32[1,512,256]{2,1,0:T(8,128)S(1)}) fusion(f32[1,2,256,256]{3,2,1,0:T(8,128)S(1)} %get-tuple-element.22, f32[1,2,256,256]{3,2,1,0:T(8,128)S(1)} %get-tuple-element.21, f32[1,1,3,512,256]{4,3,2,1,0:T(8,128)} %param.13), kind=kLoop, calls=%fused_computation.50 | loop fusion | flops 786432 | bytes 2621440 | tf_op jit(solution)/shard_map/add | solution.py:22
  65.5 1.9 %collective-permute-start.1 = (f32[2,256,256]{2,1,0:T(8,128)S(1)}, f32[2,256,256]{2,1,0:T(8,128)S(1)}, u32[]{:S(2)}, u32[]{:S(2)}) collective-permute-start(f32[2,256,256]{2,1,0:T(8,128)S(1)} %fusion.17), channel_id=1, source_target_pairs={{0,8},{4,12},{8,0},{12,4},{16,24},{20,28},{24,16},{28,20},{1,9},{5... | collective-permute-start | bytes 1572872 | tf_op jit(solution)/shard_map/ppermute | solution.py:13
  67.4 11.1 %collective-permute-done.1 = f32[2,256,256]{2,1,0:T(8,128)S(1)} collective-permute-done((f32[2,256,256]{2,1,0:T(8,128)S(1)}, f32[2,256,256]{2,1,0:T(8,128)S(1)}, u32[]{:S(2)}, u32[]{:S(2)}) %collective-permute-start.1) | collective-permute-done | bytes 524320 | tf_op jit(solution)/shard_map/ppermute | solution.py:13
  78.5 0.1 broadcast_select_fusion.1
  78.6 1.8 %convolution_bitcast_fusion.1 = f32[2,2,256,256]{3,2,1,0:T(8,128)S(1)} fusion(f32[2,256,256]{2,1,0:T(8,128)S(1)} %get-tuple-element.14, f32[2,256,256]{2,1,0:T(8,128)S(1)} %get-tuple-element.13, f32[2,512,256]{2,1,0:T(8,128)S(1)} %copy-done), kind=kOutput, calls=%fused_computation.5 | convolution fusion | flops 1610874880 | bytes 3145728 | tf_op jit(solution)/shard_map/rqk,skj->rsqj/dot_general | solution.py:72
  80.4 0.1 fusion.36
  80.5 3.4 %fusion.22 = (f32[1,512,256]{2,1,0:T(8,128)S(1)}, f32[1,512,256]{2,1,0:T(8,128)S(1)}) fusion(f32[1,2,256,256]{3,2,1,0:T(8,128)S(1)} %get-tuple-element.20, f32[1,2,256,256]{3,2,1,0:T(8,128)S(1)} %get-tuple-element.19, f32[1,1,3,512,256]{4,3,2,1,0:T(8,128)} %param.13), kind=kLoop, calls=%fused_computation.44 | loop fusion | flops 786432 | bytes 2621440 | tf_op jit(solution)/shard_map/add | solution.py:22
  83.9 2.6 %collective-permute-start.2 = (f32[2,256,256]{2,1,0:T(8,128)S(1)}, f32[2,256,256]{2,1,0:T(8,128)S(1)}, u32[]{:S(2)}, u32[]{:S(2)}) collective-permute-start(f32[2,256,256]{2,1,0:T(8,128)S(1)} %fusion.15), channel_id=1, source_target_pairs={{0,16},{4,20},{8,24},{12,28},{16,0},{20,4},{24,8},{28,12},{1,17},{... | collective-permute-start | bytes 1572872 | tf_op jit(solution)/shard_map/ppermute | solution.py:13
  86.5 21.6 %collective-permute-done.2 = f32[2,256,256]{2,1,0:T(8,128)S(1)} collective-permute-done((f32[2,256,256]{2,1,0:T(8,128)S(1)}, f32[2,256,256]{2,1,0:T(8,128)S(1)}, u32[]{:S(2)}, u32[]{:S(2)}) %collective-permute-start.2) | collective-permute-done | bytes 524320 | tf_op jit(solution)/shard_map/ppermute | solution.py:13
  108.1 0.1 broadcast_select_fusion.3
  108.2 1.8 %convolution_bitcast_fusion = f32[2,2,256,256]{3,2,1,0:T(8,128)S(1)} fusion(f32[2,256,256]{2,1,0:T(8,128)S(1)} %get-tuple-element.12, f32[2,256,256]{2,1,0:T(8,128)S(1)} %get-tuple-element.11, f32[2,512,256]{2,1,0:T(8,128)S(1)} %copy-done), kind=kOutput, calls=%fused_computation.4 | convolution fusion | flops 1610874880 | bytes 3145728 | tf_op jit(solution)/shard_map/rqk,skj->rsqj/dot_general | solution.py:72
  110.1 0.1 fusion.35
  110.1 3.4 %fusion.19 = (f32[1,512,256]{2,1,0:T(8,128)S(1)}, f32[1,512,256]{2,1,0:T(8,128)S(1)}) fusion(f32[1,2,256,256]{3,2,1,0:T(8,128)S(1)} %get-tuple-element.18, f32[1,2,256,256]{3,2,1,0:T(8,128)S(1)} %get-tuple-element.17, f32[1,1,3,512,256]{4,3,2,1,0:T(8,128)} %param.13), kind=kLoop, calls=%fused_computation.37 | loop fusion | flops 786432 | bytes 2621440 | tf_op jit(solution)/shard_map/sub | solution.py:22
  113.5 1.0 maximum_bitcast_fusion.6
  (9 shorter events, 0.1 us)
Async XLA Ops:
  0.0 60.1 %copy-start = (f32[2,512,256]{2,1,0:T(8,128)S(1)}, f32[2,512,256]{2,1,0:T(8,128)}, u32[]{:S(2)}) copy-start(f32[2,512,256]{2,1,0:T(8,128)} %param.12) | copy-start | bytes 3145732
  10.4 4.4 %copy-start.1 = (s32[1,1,4,256]{3,2,1,0:T(4,128)S(1)}, s32[1,1,4,256]{3,2,1,0:T(4,128)}, u32[]{:S(2)}) copy-start(s32[1,1,4,256]{3,2,1,0:T(4,128)} %param.10) | copy-start | bytes 12292
  10.4 30.2 %all-to-all-start = ((f32[4,256,512]{2,1,0:T(8,128)}), f32[4,256,512]{2,1,0:T(8,128)S(1)}, u32[]{:S(2)}, u32[]{:S(2)}) async-start(f32[4,256,512]{2,1,0:T(8,128)} %bitcast.140), calls=%async_computation | async-start | bytes 4194304 | tf_op jit(solution)/shard_map/all_to_all | solution.py:53
  46.1 13.9 %collective-permute-start = (f32[2,256,256]{1,2,0:T(8,128)S(1)}, f32[2,256,256]{1,2,0:T(8,128)S(1)}, u32[]{:S(2)}, u32[]{:S(2)}) collective-permute-start(f32[2,256,256]{1,2,0:T(8,128)S(1)} %dynamic-slice_bitcast_fusion), channel_id=1, source_target_pairs={{0,4},{4,0},{8,12},{12,8},{16,20},{20,16},{24,28},{28,24},{1,5},{5... | collective-permute-start | bytes 1572872 | tf_op jit(solution)/shard_map/ppermute | solution.py:13
  65.5 13.0 %collective-permute-start.1 = (f32[2,256,256]{2,1,0:T(8,128)S(1)}, f32[2,256,256]{2,1,0:T(8,128)S(1)}, u32[]{:S(2)}, u32[]{:S(2)}) collective-permute-start(f32[2,256,256]{2,1,0:T(8,128)S(1)} %fusion.17), channel_id=1, source_target_pairs={{0,8},{4,12},{8,0},{12,4},{16,24},{20,28},{24,16},{28,20},{1,9},{5... | collective-permute-start | bytes 1572872 | tf_op jit(solution)/shard_map/ppermute | solution.py:13
  83.9 24.2 %collective-permute-start.2 = (f32[2,256,256]{2,1,0:T(8,128)S(1)}, f32[2,256,256]{2,1,0:T(8,128)S(1)}, u32[]{:S(2)}, u32[]{:S(2)}) collective-permute-start(f32[2,256,256]{2,1,0:T(8,128)S(1)} %fusion.15), channel_id=1, source_target_pairs={{0,16},{4,20},{8,24},{12,28},{16,0},{20,4},{24,8},{28,12},{1,17},{... | collective-permute-start | bytes 1572872 | tf_op jit(solution)/shard_map/ppermute | solution.py:13
where the time goes:
time: 115 us
  waiting for transfers between devices  70.2 us (61%)
  other arithmetic  15.2 us (13%)
  matrix products  11.3 us (10%)
  starting transfers between devices  11 us (10%)
  local copies, waits for them, and re-layouts  6.02 us (5%)
    ppermute x3, waiting for transfers between devices, swapped(): lax.ppermute(x, axis, [(i, i ^ 1 << bit) for i in range(lax.axis_size(axi...  44.4 us
    all_to_all x1, waiting for transfers between devices, shards(): lax.all_to_all(outgoing.reshape(param_count, slot_count, 2 * weight_count...  25.8 us
    add x2, other arithmetic, rotate(): real_part * sine_part + imag_part * cosine  6.75 us
    ppermute x3, starting transfers between devices, swapped(): lax.ppermute(x, axis, [(i, i ^ 1 << bit) for i in range(lax.axis_size(axi...  6.66 us
    dot_general x3, matrix products, shards(): jnp.einsum('rqk,skj->rsqj', joined, interp, precision=HIGH)  5.54 us
    all_to_all x1, starting transfers between devices, shards(): lax.all_to_all(outgoing.reshape(param_count, slot_count, 2 * weight_count...  4.37 us
    scatter x1, local copies, waits for them, and re-layouts, shards(): outgoing = jnp.zeros((param_count * slot_count, 2 * weight_count), jnp.fl...  3.67 us
    dot_general x1, matrix products, shards(): jnp.dot(selector, arrived.reshape(-1, 2 * weight_count), precision=HIGH)  3.55 us
  transfers between devices with their start and end apart: 4, of which 4 were waited for; matrix products, arithmetic and copies ran while one was open for 0% of the time, Pallas kernels for 0%

commit v1 on v0

v1 whole, which is shorter than its diff:
```python
import functools

import jax
import jax.numpy as jnp
from jax import lax
from jax.experimental import pallas as pl
from jax.experimental.pallas import tpu as pltpu
from jax.sharding import PartitionSpec as P

LEVELS = 3
CHUNKS = 4
MESH = pl.DeviceIdType.MESH
F32 = jnp.float32
BF16 = jnp.bfloat16

SIN_TERMS = (-1 / 6, 1 / 120, -1 / 5040, 1 / 362880, -1 / 39916800)
COS_TERMS = (-1 / 2, 1 / 24, -1 / 720, 1 / 40320, -1 / 3628800, 1 / 479001600)


def split(x):
    high = x.astype(BF16)
    return high, (x - high.astype(F32)).astype(BF16)


def dot(a, b):
    return jnp.dot(a, b, preferred_element_type=F32)


def dot3(a, b):
    return dot(a[0], b[0]) + (dot(a[0], b[1]) + dot(a[1], b[0]))


def flag(condition):
    return jnp.where(condition, 1.0, 0.0).astype(BF16)


def flipped(index, mask):
    out = index
    bit = 1
    while bit <= mask:
        if mask & bit:
            out = out + bit * (1 - 2 * ((index // bit) % 2))
        bit *= 2
    return out


def sin_cos(x):
    h = x * 0.5
    y = h * h
    s = jnp.full_like(y, SIN_TERMS[-1])
    for term in SIN_TERMS[-2::-1]:
        s = s * y + term
    s = h + h * (y * s)
    c = jnp.full_like(y, COS_TERMS[-1])
    for term in COS_TERMS[-2::-1]:
        c = c * y + term
    c = 1.0 + y * c
    return 2.0 * s * c, 1.0 - 2.0 * s * s


def kernel(
    param_count,
    traces,
    owners,
    counts,
    pairs,
    anterp,
    interp,
    phase,
    out,
    going,
    arrived,
    selector,
    first_map,
    level_map,
    cosines,
    sines,
    send0,
    recv0,
    kept0,
    send,
    recv,
    kept,
    gather_send,
    gather_recv,
    level_send,
    level_recv,
):
    box = lax.axis_index("box")
    me = lax.axis_index("param")
    rows_total, samples = traces.shape
    slots = pairs.shape[1]
    weights = interp.shape[2]
    half = phase.shape[1] // 2
    rows = half // CHUNKS
    bits = [(box // 2**level) % 2 for level in range(LEVELS)]
    partners = [flipped(box, 2**level) for level in range(LEVELS)]
    peers = [flipped(me, j) for j in range(param_count)]

    barrier = pltpu.get_barrier_semaphore()
    for j in range(1, param_count):
        pl.semaphore_signal(barrier, inc=1, device_id=(box, peers[j]), device_id_type=MESH)
    for level in range(LEVELS):
        pl.semaphore_signal(barrier, inc=1, device_id=(partners[level], me), device_id_type=MESH)

    owner = owners[...]
    owner_rows = max(param_count, 16)
    named = owner == lax.broadcasted_iota(jnp.int32, (owner_rows, rows_total), 0)
    before = flag(
        lax.broadcasted_iota(jnp.int32, (rows_total, rows_total), 0)
        < lax.broadcasted_iota(jnp.int32, (rows_total, rows_total), 1)
    )
    running = dot(flag(named), before)
    rank = jnp.sum(jnp.where(named, running, 0.0), axis=0, keepdims=True).astype(jnp.int32)
    live = lax.broadcasted_iota(jnp.int32, (1, rows_total), 1) < counts[0, 0]
    masked = split(traces[...])
    slot_ids = lax.broadcasted_iota(jnp.int32, (slots, rows_total), 0)

    def block_for(target):
        key = jnp.where((owner == target) & live, rank, -1)
        chosen = flag(slot_ids == key)
        return dot(chosen, masked[0]) + dot(chosen, masked[1])

    pl.semaphore_wait(barrier, param_count - 1 + LEVELS)
    gathers = []
    for j in range(param_count - 1, 0, -1):
        going[j - 1] = block_for(peers[j])
        copy = pltpu.make_async_remote_copy(
            src_ref=going.at[j - 1],
            dst_ref=arrived.at[j - 1],
            send_sem=gather_send.at[j - 1],
            recv_sem=gather_recv.at[j - 1],
            device_id=(box, peers[j]),
            device_id_type=MESH,
        )
        copy.start()
        gathers.append((j, copy))
    own_block = split(block_for(me))

    pair_ids = lax.broadcasted_iota(jnp.int32, (half, slots), 0)
    for j in range(param_count):
        table = pairs[pl.ds(peers[j], 1), :]
        selector[j, 0] = flag(pair_ids + (1 - bits[0]) * half == table)
        selector[j, 1] = flag(pair_ids + bits[0] * half == table)

    for side in range(2):
        for s in range(2):
            piece = split(interp[s, side * weights : (side + 1) * weights, :])
            level_map[0, side, s] = piece[0]
            level_map[1, side, s] = piece[1]
            for r in range(2):
                product = dot3(split(anterp[:, r * weights : (r + 1) * weights]), piece)
                high, low = split(product)
                first_map[0, side, s, :, r * weights : (r + 1) * weights] = high
                first_map[1, side, s, :, r * weights : (r + 1) * weights] = low

    for level in range(LEVELS):
        def angles(step, carry):
            at = pl.ds(pl.multiple_of(step * 16, 16), 16)
            sine, cosine = sin_cos(phase[level, at, :])
            sines[level, at, :] = sine
            cosines[level, at, :] = cosine
            return carry

        lax.fori_loop(0, 2 * half // 16, angles, 0, unroll=2)

    blocks = [(0, own_block)]
    for j, copy in gathers[::-1]:
        copy.wait_recv()
        blocks.append((j, split(arrived[j - 1])))

    def summed(which):
        total = None
        for j, (high, low) in blocks:
            chosen = selector[j, which]
            part = dot(chosen, high) + dot(chosen, low)
            total = part if total is None else total + part
        return total

    def exchange(level, i, source, target):
        copy = pltpu.make_async_remote_copy(
            src_ref=source,
            dst_ref=target,
            send_sem=level_send.at[level, i],
            recv_sem=level_recv.at[level, i],
            device_id=(partners[level], me),
            device_id_type=MESH,
        )
        copy.start()
        return copy

    copies = {}
    send0[...] = summed(0)
    for i in range(CHUNKS):
        at = pl.ds(i * rows, rows)
        copies[0, i] = exchange(0, i, send0.at[at], recv0.at[at])
    kept0[...] = summed(1)

    def turned(level, s, i, real, imag):
        at = pl.ds(pl.multiple_of(s * half + i * rows, rows), rows)
        cosine = cosines[level, at, :]
        sine = sines[level, at, :]
        return real * cosine - imag * sine, real * sine + imag * cosine

    def combined(level, i, s, mine, other):
        side = bits[level]
        if level == 0:
            both = dot3(mine, (first_map[0, side, s], first_map[1, side, s])) + dot3(
                other, (first_map[0, 1 - side, s], first_map[1, 1 - side, s])
            )
            real, imag = both[:, :weights], both[:, weights:]
        else:
            both = dot3(mine, (level_map[0, side, s], level_map[1, side, s])) + dot3(
                other, (level_map[0, 1 - side, s], level_map[1, 1 - side, s])
            )
            real, imag = both[:rows], both[rows:]
        return turned(level, s, i, real, imag)

    def step(level, i):
        copies[level, i].wait_recv()
        if level == 0:
            at = pl.ds(i * rows, rows)
            mine, other = split(kept0[at, :]), split(recv0[at, :])
        else:
            mine = split(kept[level - 1, i].reshape(2 * rows, weights))
            other = split(recv[level - 1, i].reshape(2 * rows, weights))
        if level < LEVELS - 1:
            bit = bits[level + 1]
            real, imag = combined(level, i, 1 - bit, mine, other)
            send[level, i, 0] = real
            send[level, i, 1] = imag
            copies[level + 1, i] = exchange(
                level + 1, i, send.at[level, i], recv.at[level, i]
            )
            real, imag = combined(level, i, bit, mine, other)
            kept[level, i, 0] = real
            kept[level, i, 1] = imag
        else:
            for s in range(2):
                real, imag = combined(level, i, s, mine, other)
                out[0, s * half + i * rows : s * half + (i + 1) * rows, :] = real
                out[1, s * half + i * rows : s * half + (i + 1) * rows, :] = imag

    for t in range(CHUNKS + 1):
        if t < CHUNKS:
            step(0, t)
        if t >= 1:
            step(1, t - 1)
    for i in range(CHUNKS):
        step(2, i)

    for _, copy in gathers:
        copy.wait_send()
    for copy in copies.values():
        copy.wait_send()


def shards(param_count, traces, owners, counts, pair_table, anterp, interp, phase):
    rows_total, samples = traces.shape[2:]
    slots = pair_table.shape[3]
    pair_count, weights = phase.shape[3:]
    half = pair_count // 2
    rows = half // CHUNKS
    vmem = pl.BlockSpec(memory_space=pltpu.VMEM)
    smem = pl.BlockSpec(memory_space=pltpu.SMEM)
    others = param_count - 1
    result = pl.pallas_call(
        functools.partial(kernel, param_count),
        out_shape=jax.ShapeDtypeStruct((2, pair_count, weights), F32),
        in_specs=[vmem, vmem, smem, vmem, vmem, vmem, vmem],
        out_specs=vmem,
        scratch_shapes=[
            pltpu.VMEM((others, slots, samples), F32),
            pltpu.VMEM((others, slots, samples), F32),
            pltpu.VMEM((param_count, 2, half, slots), BF16),
            pltpu.VMEM((2, 2, 2, samples, 2 * weights), BF16),
            pltpu.VMEM((2, 2, 2, weights, weights), BF16),
            pltpu.VMEM((LEVELS, pair_count, weights), F32),
            pltpu.VMEM((LEVELS, pair_count, weights), F32),
            pltpu.VMEM((half, samples), F32),
            pltpu.VMEM((half, samples), F32),
            pltpu.VMEM((half, samples), F32),
            pltpu.VMEM((LEVELS - 1, CHUNKS, 2, rows, weights), F32),
            pltpu.VMEM((LEVELS - 1, CHUNKS, 2, rows, weights), F32),
            pltpu.VMEM((LEVELS - 1, CHUNKS, 2, rows, weights), F32),
            pltpu.SemaphoreType.DMA((others,)),
            pltpu.SemaphoreType.DMA((others,)),
            pltpu.SemaphoreType.DMA((LEVELS, CHUNKS)),
            pltpu.SemaphoreType.DMA((LEVELS, CHUNKS)),
        ],
        compiler_params=pltpu.CompilerParams(
            collective_id=0, has_side_effects=True, vmem_limit_bytes=50 * 2**20
        ),
    )(
        traces[0, 0],
        owners.reshape(1, rows_total),
        counts,
        pair_table[0, 0],
        anterp,
        interp,
        phase[0, 0],
    )
    return result[None, None]


def solution(mesh):
    placed = (
        P("box", "param", None, None),
        P("box", "param", None, None),
        P("box", "param"),
        P("box", "param", None, None),
        P(),
        P(),
        P("box", "param", None, None, None),
    )
    return jax.shard_map(
        functools.partial(shards, mesh.shape["param"]),
        mesh=mesh,
        in_specs=placed,
        out_specs=P("box", "param", None, None, None),
        check_vma=False,
    )
```

time: 115 us -> 59.1 us (0.51)
  waiting for transfers between devices: 70.2 us -> 0 us
  Pallas kernels: 0 us -> 52.4 us
  other arithmetic: 15.2 us -> 0 us
  matrix products: 11.3 us -> 0 us
  starting transfers between devices: 11 us -> 0 us
    pallas_call x0 -> x1, Pallas kernels: none -> 52.4 us  [shards(): pl.pallas_call(functools.partial(kernel, param_count), out_shape=jax.Shap...]
    ppermute x3 -> x0, waiting for transfers between devices: 44.4 us -> none  [swapped(): lax.ppermute(x, axis, [(i, i ^ 1 << bit) for i in range(lax.axis_size(axi...]
    all_to_all x1 -> x0, waiting for transfers between devices: 25.8 us -> none  [shards(): lax.all_to_all(outgoing.reshape(param_count, slot_count, 2 * weight_count...]
    dot_general x5 -> x0, matrix products: 11.3 us -> none  [the longest x3 5.54 us: shards(): jnp.einsum('rqk,skj->rsqj', joined, interp, precision=HIGH)]
    add x2 -> x0, other arithmetic: 6.75 us -> none  [rotate(): real_part * sine_part + imag_part * cosine]
    ppermute x3 -> x0, starting transfers between devices: 6.66 us -> none  [swapped(): lax.ppermute(x, axis, [(i, i ^ 1 << bit) for i in range(lax.axis_size(axi...]
    unnamed x5 -> x11, local copies, waits for them, and re-layouts: 0.01 us -> 5.64 us
    all_to_all x1 -> x0, starting transfers between devices: 4.37 us -> none  [shards(): lax.all_to_all(outgoing.reshape(param_count, slot_count, 2 * weight_count...]
  transfers between devices with their start and end apart: 4 -> 0, of which waited for: 4 -> 0; matrix products, arithmetic and copies ran while one was open for 0% -> 0% of each run, Pallas kernels for 0% -> 0%
where the time goes in v1:
time: 59.1 us; the launch traced here: 58.7 us
  Pallas kernels  52.4 us (89%)
  local copies, waits for them, and re-layouts  5.64 us (10%)
  between operations  0.67 us (1%)
    pallas_call x1, Pallas kernels, shards(): pl.pallas_call(functools.partial(kernel, param_count), out_shape=jax.Shap...  52.4 us
    unnamed x11, local copies, waits for them, and re-layouts  5.64 us

profile of v1, /device:TPU:0, one launch (start us, length us, event | category | flops | bytes accessed | tf_op | source)
XLA Modules:
  0.0 58.7 jit_solution(14716043120027844736)
XLA Ops:
  0.7 0.0 copy-start
  0.7 1.2 %copy-done = f32[2,512,256]{2,1,0:T(8,128)S(1)} copy-done((f32[2,512,256]{2,1,0:T(8,128)S(1)}, f32[2,512,256]{2,1,0:T(8,128)}, u32[]{:S(2)}) %copy-start) | copy-done | bytes 1048600
  1.9 0.0 copy-start.1
  1.9 1.0 %copy-done.1 = f32[1,1,512,256]{3,2,1,0:T(8,128)S(1)} copy-done((f32[1,1,512,256]{3,2,1,0:T(8,128)S(1)}, f32[1,1,512,256]{3,2,1,0:T(8,128)}, u32[]{:S(2)}) %copy-start.1) | copy-done | bytes 524312
  2.9 0.0 copy-start.2
  2.9 1.0 %copy-done.2 = f32[256,512]{1,0:T(8,128)S(1)} copy-done((f32[256,512]{1,0:T(8,128)S(1)}, f32[256,512]{1,0:T(8,128)}, u32[]{:S(2)}) %copy-start.2) | copy-done | bytes 524312
  4.0 0.0 copy-start.3
  4.0 0.7 %copy-done.3 = s32[1,1,4,256]{3,2,1,0:T(4,128)S(1)} copy-done((s32[1,1,4,256]{3,2,1,0:T(4,128)S(1)}, s32[1,1,4,256]{3,2,1,0:T(4,128)}, u32[]{:S(2)}) %copy-start.3) | copy-done | bytes 4120
  4.6 0.0 copy-start.4
  4.7 0.7 %copy-done.4 = s32[1,1,512,1]{2,3,1,0:T(1,128)S(1)} copy-done((s32[1,1,512,1]{2,3,1,0:T(1,128)S(1)}, s32[1,1,512,1]{2,3,1,0:T(1,128)}, u32[]{:S(2)}) %copy-start.4) | copy-done | bytes 2072
  5.3 52.4 %shard_map.73 = f32[2,512,256]{2,1,0:T(8,128)S(1)} custom-call(f32[512,256]{1,0:T(8,128)S(1)} %bitcast.6, s32[1,512]{1,0:T(1,128)S(1)} %bitcast.8, s32[1,1]{1,0:T(1,128)S(6)} %copy.9.counts, s32[4,256]{1,0:T(4,128)S(1)} %bitcast.7, f32[256,512]{1,0:T(8,128)S(1)} %copy-done.2, f32[2,512,256]{2,1,0:T(8,128)S(1)} %copy-done, f32[3,512,256]{2,1,0:T(8,128)} %bitcast.9), custom_call_target="tpu_custom_call" | custom-call | tf_op jit(solution)/shard_map/pallas_call | solution.py:267
  57.8 1.0 %copy.10 = f32[1,1,2,512,256]{4,3,2,1,0:T(8,128)} copy(f32[1,1,2,512,256]{4,3,2,1,0:T(8,128)S(1)} %bitcast.5) | data formatting | bytes 2097152
Async XLA Ops:
  0.7 1.2 %copy-start = (f32[2,512,256]{2,1,0:T(8,128)S(1)}, f32[2,512,256]{2,1,0:T(8,128)}, u32[]{:S(2)}) copy-start(f32[2,512,256]{2,1,0:T(8,128)} %interp.1) | copy-start | bytes 3145732
  1.9 1.0 %copy-start.1 = (f32[1,1,512,256]{3,2,1,0:T(8,128)S(1)}, f32[1,1,512,256]{3,2,1,0:T(8,128)}, u32[]{:S(2)}) copy-start(f32[1,1,512,256]{3,2,1,0:T(8,128)} %param.7) | copy-start | bytes 1572868
  2.9 1.0 %copy-start.2 = (f32[256,512]{1,0:T(8,128)S(1)}, f32[256,512]{1,0:T(8,128)}, u32[]{:S(2)}) copy-start(f32[256,512]{1,0:T(8,128)} %anterp.1) | copy-start | bytes 1572868
  4.0 0.7 %copy-start.3 = (s32[1,1,4,256]{3,2,1,0:T(4,128)S(1)}, s32[1,1,4,256]{3,2,1,0:T(4,128)}, u32[]{:S(2)}) copy-start(s32[1,1,4,256]{3,2,1,0:T(4,128)} %param.10) | copy-start | bytes 12292
  4.6 0.7 %copy-start.4 = (s32[1,1,512,1]{2,3,1,0:T(1,128)S(1)}, s32[1,1,512,1]{2,3,1,0:T(1,128)}, u32[]{:S(2)}) copy-start(s32[1,1,512,1]{2,3,1,0:T(1,128)} %param.8) | copy-start | bytes 6148

commit v2 on v1

--- a/solution.py
+++ b/solution.py
@@ -8,7 +8,8 @@
 from jax.sharding import PartitionSpec as P
 
 LEVELS = 3
-CHUNKS = 4
+CHUNKS = 8
+LAG = 1
 MESH = pl.DeviceIdType.MESH
 F32 = jnp.float32
 BF16 = jnp.bfloat16
@@ -60,14 +61,19 @@
 
 def kernel(
     param_count,
-    traces,
+    traces_hbm,
     owners,
     counts,
     pairs,
+    anterp_hbm,
+    interp_hbm,
+    phase_hbm,
+    out_hbm,
+    out,
+    traces,
     anterp,
     interp,
     phase,
-    out,
     going,
     arrived,
     selector,
@@ -81,11 +87,27 @@
     send,
     recv,
     kept,
+    load_sem,
+    store_sem,
     gather_send,
     gather_recv,
     level_send,
     level_recv,
 ):
+    loads = [
+        pltpu.make_async_copy(source, target, load_sem.at[k])
+        for k, (source, target) in enumerate(
+            [
+                (traces_hbm, traces),
+                (anterp_hbm, anterp),
+                (interp_hbm, interp),
+                (phase_hbm, phase),
+            ]
+        )
+    ]
+    for load in loads:
+        load.start()
+
     box = lax.axis_index("box")
     me = lax.axis_index("param")
     rows_total, samples = traces.shape
@@ -113,6 +135,7 @@
     running = dot(flag(named), before)
     rank = jnp.sum(jnp.where(named, running, 0.0), axis=0, keepdims=True).astype(jnp.int32)
     live = lax.broadcasted_iota(jnp.int32, (1, rows_total), 1) < counts[0, 0]
+    loads[0].wait()
     masked = split(traces[...])
     slot_ids = lax.broadcasted_iota(jnp.int32, (slots, rows_total), 0)
 
@@ -143,6 +166,8 @@
         selector[j, 0] = flag(pair_ids + (1 - bits[0]) * half == table)
         selector[j, 1] = flag(pair_ids + bits[0] * half == table)
 
+    loads[1].wait()
+    loads[2].wait()
     for side in range(2):
         for s in range(2):
             piece = split(interp[s, side * weights : (side + 1) * weights, :])
@@ -154,6 +179,7 @@
                 first_map[0, side, s, :, r * weights : (r + 1) * weights] = high
                 first_map[1, side, s, :, r * weights : (r + 1) * weights] = low
 
+    loads[3].wait()
     for level in range(LEVELS):
         def angles(step, carry):
             at = pl.ds(pl.multiple_of(step * 16, 16), 16)
@@ -164,18 +190,22 @@
 
         lax.fori_loop(0, 2 * half // 16, angles, 0, unroll=2)
 
-    blocks = [(0, own_block)]
+    def part(j, which, at, values):
+        chosen = selector[j, which, at, :]
+        return dot(chosen, values[0]) + dot(chosen, values[1])
+
+    every = pl.ds(0, half)
+    send0[...] = part(0, 0, every, own_block)
+    kept0[...] = part(0, 1, every, own_block)
+    blocks = []
     for j, copy in gathers[::-1]:
         copy.wait_recv()
-        blocks.append((j, split(arrived[j - 1])))
-
-    def summed(which):
-        total = None
-        for j, (high, low) in blocks:
-            chosen = selector[j, which]
-            part = dot(chosen, high) + dot(chosen, low)
-            total = part if total is None else total + part
-        return total
+        block = split(arrived[j - 1])
+        if j == 1:
+            send0[...] += part(j, 0, every, block)
+            kept0[...] += part(j, 1, every, block)
+        else:
+            blocks.append((j, block))
 
     def exchange(level, i, source, target):
         copy = pltpu.make_async_remote_copy(
@@ -190,11 +220,14 @@
         return copy
 
     copies = {}
-    send0[...] = summed(0)
+    stores = []
     for i in range(CHUNKS):
         at = pl.ds(i * rows, rows)
+        for j, block in blocks:
+            send0[at, :] += part(j, 0, at, block)
         copies[0, i] = exchange(0, i, send0.at[at], recv0.at[at])
-    kept0[...] = summed(1)
+    for j, block in blocks:
+        kept0[...] += part(j, 1, every, block)
 
     def turned(level, s, i, real, imag):
         at = pl.ds(pl.multiple_of(s * half + i * rows, rows), rows)
@@ -238,17 +271,26 @@
         else:
             for s in range(2):
                 real, imag = combined(level, i, s, mine, other)
-                out[0, s * half + i * rows : s * half + (i + 1) * rows, :] = real
-                out[1, s * half + i * rows : s * half + (i + 1) * rows, :] = imag
-
-    for t in range(CHUNKS + 1):
+                at = pl.ds(s * half + i * rows, rows)
+                out[0, at, :] = real
+                out[1, at, :] = imag
+                for r in range(2):
+                    store = pltpu.make_async_copy(
+                        out.at[r, at], out_hbm.at[r, at], store_sem.at[i, s, r]
+                    )
+                    store.start()
+                    stores.append(store)
+
+    for t in range(CHUNKS + LAG):
         if t < CHUNKS:
             step(0, t)
-        if t >= 1:
-            step(1, t - 1)
+        if t >= LAG:
+            step(1, t - LAG)
     for i in range(CHUNKS):
         step(2, i)
 
+    for store in stores:
+        store.wait()
     for _, copy in gathers:
         copy.wait_send()
     for copy in copies.values():
@@ -263,13 +305,19 @@
     rows = half // CHUNKS
     vmem = pl.BlockSpec(memory_space=pltpu.VMEM)
     smem = pl.BlockSpec(memory_space=pltpu.SMEM)
+    hbm = pl.BlockSpec(memory_space=pltpu.HBM)
     others = param_count - 1
     result = pl.pallas_call(
         functools.partial(kernel, param_count),
         out_shape=jax.ShapeDtypeStruct((2, pair_count, weights), F32),
-        in_specs=[vmem, vmem, smem, vmem, vmem, vmem, vmem],
-        out_specs=vmem,
+        in_specs=[hbm, vmem, smem, vmem, hbm, hbm, hbm],
+        out_specs=hbm,
         scratch_shapes=[
+            pltpu.VMEM((2, pair_count, weights), F32),
+            pltpu.VMEM((rows_total, samples), F32),
+            pltpu.VMEM(anterp.shape, F32),
+            pltpu.VMEM(interp.shape, F32),
+            pltpu.VMEM((LEVELS, pair_count, weights), F32),
             pltpu.VMEM((others, slots, samples), F32),
             pltpu.VMEM((others, slots, samples), F32),
             pltpu.VMEM((param_count, 2, half, slots), BF16),
@@ -283,13 +331,15 @@
             pltpu.VMEM((LEVELS - 1, CHUNKS, 2, rows, weights), F32),
             pltpu.VMEM((LEVELS - 1, CHUNKS, 2, rows, weights), F32),
             pltpu.VMEM((LEVELS - 1, CHUNKS, 2, rows, weights), F32),
+            pltpu.SemaphoreType.DMA((4,)),
+            pltpu.SemaphoreType.DMA((CHUNKS, 2, 2)),
             pltpu.SemaphoreType.DMA((others,)),
             pltpu.SemaphoreType.DMA((others,)),
             pltpu.SemaphoreType.DMA((LEVELS, CHUNKS)),
             pltpu.SemaphoreType.DMA((LEVELS, CHUNKS)),
         ],
         compiler_params=pltpu.CompilerParams(
-            collective_id=0, has_side_effects=True, vmem_limit_bytes=50 * 2**20
+            collective_id=0, has_side_effects=True, vmem_limit_bytes=60 * 2**20
         ),
     )(
         traces[0, 0],

time: 59.1 us -> 54.8 us (0.927)
  local copies, waits for them, and re-layouts: 5.64 us -> 2.26 us
  Pallas kernels: 52.4 us -> 51.7 us
    unnamed x11 -> x1, local copies, waits for them, and re-layouts: 5.64 us -> 2.26 us
    pallas_call x1, Pallas kernels: 52.4 us -> 51.7 us  [shards(): pl.pallas_call(functools.partial(kernel, param_count), out_shape=jax.Shap...]
where the time goes in v2:
time: 54.8 us; the launch traced here: 54.6 us
  Pallas kernels  51.7 us (94%)
  local copies, waits for them, and re-layouts  2.26 us (4%)
  between operations  0.66 us (1%)
    pallas_call x1, Pallas kernels, shards(): pl.pallas_call(functools.partial(kernel, param_count), out_shape=jax.Shap...  51.7 us
    unnamed x1, local copies, waits for them, and re-layouts  2.26 us

profile of v2, /device:TPU:0, one launch (start us, length us, event | category | flops | bytes accessed | tf_op | source)
XLA Modules:
  0.0 54.6 jit_solution(517858120611284586)
XLA Ops:
  0.7 51.7 %shard_map.73 = f32[2,512,256]{2,1,0:T(8,128)} custom-call(f32[512,256]{1,0:T(8,128)} %bitcast.7, s32[1,512]{1,0:T(1,128)} %bitcast.9, s32[1,1]{1,0:T(1,128)S(6)} %copy.9.counts, s32[4,256]{1,0:T(4,128)} %bitcast.8, f32[256,512]{1,0:T(8,128)} %anterp_hbm.1, f32[2,512,256]{2,1,0:T(8,128)} %interp_hbm.1, f32[3,512,256]{2,1,0:T(8,128)} %bitcast.6), custom_call_target="tpu_custom_call" | custom-call | tf_op jit(solution)/shard_map/pallas_call | solution.py:310
  52.3 2.3 %copy.10 = f32[1,1,2,512,256]{4,3,2,1,0:T(8,128)} copy(f32[1,1,2,512,256]{4,3,2,1,0:T(8,128)} %bitcast.5) | data formatting | bytes 2097152

commit v3 on v2

--- a/solution.py
+++ b/solution.py
@@ -249,6 +249,17 @@
             real, imag = both[:rows], both[rows:]
         return turned(level, s, i, real, imag)
 
+    def keep(level, i, mine, other):
+        real, imag = combined(level, i, bits[level + 1], mine, other)
+        kept[level, i, 0] = real
+        kept[level, i, 1] = imag
+
+    def operands(level, i):
+        return (
+            split(kept[level - 1, i].reshape(2 * rows, weights)),
+            split(recv[level - 1, i].reshape(2 * rows, weights)),
+        )
+
     def step(level, i):
         copies[level, i].wait_recv()
         if level == 0:
@@ -265,9 +276,8 @@
             copies[level + 1, i] = exchange(
                 level + 1, i, send.at[level, i], recv.at[level, i]
             )
-            real, imag = combined(level, i, bit, mine, other)
-            kept[level, i, 0] = real
-            kept[level, i, 1] = imag
+            if level == 0:
+                keep(level, i, mine, other)
         else:
             for s in range(2):
                 real, imag = combined(level, i, s, mine, other)
@@ -286,6 +296,8 @@
             step(0, t)
         if t >= LAG:
             step(1, t - LAG)
+    for i in range(CHUNKS):
+        keep(1, i, *operands(1, i))
     for i in range(CHUNKS):
         step(2, i)
 

time: 54.8 us -> 56.7 us (1.035)
  Pallas kernels: 51.7 us -> 53.6 us
    pallas_call x1, Pallas kernels: 51.7 us -> 53.6 us  [shards(): pl.pallas_call(functools.partial(kernel, param_count), out_shape=jax.Shap...]
where the time goes in v3:
time: 56.7 us; the launch traced here: 56.5 us
  Pallas kernels  53.6 us (95%)
  local copies, waits for them, and re-layouts  2.26 us (4%)
  between operations  0.66 us (1%)
    pallas_call x1, Pallas kernels, shards(): pl.pallas_call(functools.partial(kernel, param_count), out_shape=jax.Shap...  53.6 us
    unnamed x1, local copies, waits for them, and re-layouts  2.26 us

profile of v3, /device:TPU:0, one launch (start us, length us, event | category | flops | bytes accessed | tf_op | source)
XLA Modules:
  0.0 56.5 jit_solution(5410951669757715120)
XLA Ops:
  0.7 53.6 %shard_map.73 = f32[2,512,256]{2,1,0:T(8,128)} custom-call(f32[512,256]{1,0:T(8,128)} %bitcast.7, s32[1,512]{1,0:T(1,128)} %bitcast.9, s32[1,1]{1,0:T(1,128)S(6)} %copy.9.counts, s32[4,256]{1,0:T(4,128)} %bitcast.8, f32[256,512]{1,0:T(8,128)} %anterp_hbm.1, f32[2,512,256]{2,1,0:T(8,128)} %interp_hbm.1, f32[3,512,256]{2,1,0:T(8,128)} %bitcast.6), custom_call_target="tpu_custom_call" | custom-call | tf_op jit(solution)/shard_map/pallas_call | solution.py:322
  54.3 2.3 %copy.10 = f32[1,1,2,512,256]{4,3,2,1,0:T(8,128)} copy(f32[1,1,2,512,256]{4,3,2,1,0:T(8,128)} %bitcast.5) | data formatting | bytes 2097152
